TPU v7x, 256 devices: a whole 4x4x8 slice. The times are simulated.
256 devices in a mesh: dp: 16 (over z_hi, y), mp: 16 (over x, z_lo, core).
Axes of the slice: x: 4, y: 4, z: 8 (z_hi: 4, z_lo: 2; z = z_hi * 2 + z_lo), core: 2. Of those that a mesh axis runs over, the one named last changes fastest.
Arguments:
- tokens: bfloat16 [2048, 8192], P('dp', 'mp'), may hold values from -6 to 6
- expand_weight: bfloat16 [32, 256, 1024], P('mp'), may hold values from -0.375 to 0.375
- section_weight: bfloat16 [4, 128, 2, 256, 256], P(None, 'mp'), may hold values from -0.25 to 0.25
- contract_weight: bfloat16 [32, 1024, 256], P('mp'), may hold values from -0.1875 to 0.1875
- pattern: int32 [4, 8], replicated, may hold values from 0 to 7, each once within a row
- cotangent: bfloat16 [2048, 8192], P('dp', 'mp'), may hold values from -6 to 6
Outputs:
- output: bfloat16 [2048, 8192], P('dp', 'mp')
- input_grad: bfloat16 [2048, 8192], P('dp', 'mp')
- expand_grad: bfloat16 [32, 256, 1024], P('mp', 'dp')
- section_grad: bfloat16 [4, 128, 2, 256, 256], P(None, 'mp', None, 'dp')
- contract_grad: bfloat16 [32, 1024, 256], P('mp', 'dp')
Inputs may be any that keep to these rules, and one draw needn't show every extreme that they name: Each row of pattern is a permutation of 0 .. 7.
All inputs are finite; a program needn't handle non-finite values.
Results may differ from a plain program's by a relative error of at most 0.025.
Values may be sent and summed in bfloat16 or wider, within the bound.
A program may use at most 128 MiB of HBM per device.

v0:
```python
import math

import jax
import jax.numpy as jnp
from jax import lax
from jax.sharding import PartitionSpec as P


def from_partner(shard, axis, apart):
    return lax.ppermute(shard, axis, [(i, i ^ 1 << apart) for i in range(lax.axis_size(axis))])


def gelu_exact(values):
    return jax.nn.gelu(values, approximate=False)


def body(tokens, expand_weight, section_weight, contract_weight, pattern, cotangent):
    tok_rows = tokens.shape[0]
    feat_blocks = expand_weight.shape[0]
    block_size = expand_weight.shape[1]
    hidden_width = expand_weight.shape[2]
    hidden_count = section_weight.shape[1]
    sections = lax.axis_size("mp").bit_length() - 1
    grad_scale = 1.0 / math.sqrt(tok_rows * lax.axis_size("dp"))
    tok_blocks = tokens.reshape(tok_rows, feat_blocks, block_size)
    hidden = jnp.einsum(
        "rmi,mio->rmo", tok_blocks, expand_weight, preferred_element_type=jnp.float32
    )
    hidden = hidden.reshape(tok_rows, hidden_count, block_size).astype(jnp.bfloat16)
    saved = []
    mixed = None
    for section in range(sections):
        chosen = jnp.take(hidden, pattern[section], axis=1)
        partner = from_partner(chosen, "mp", section)
        paired = jnp.stack([chosen, partner], axis=2)
        saved.append(paired)
        mixed = jnp.einsum(
            "rlsc,lscd->rld", paired, section_weight[section], preferred_element_type=jnp.float32
        )
        if section + 1 < sections:
            hidden = mixed.astype(jnp.bfloat16)
    activated, gelu_back = jax.vjp(gelu_exact, mixed)
    activated = activated.astype(jnp.bfloat16)
    gelu_blocks = activated.reshape(tok_rows, feat_blocks, hidden_width)
    output = jnp.einsum(
        "rje,jed->rjd", gelu_blocks, contract_weight, preferred_element_type=jnp.float32
    )
    output = output.reshape(tok_rows, feat_blocks * block_size).astype(jnp.bfloat16)
    cot_blocks = cotangent.reshape(tok_rows, feat_blocks, block_size)
    contract_term = jnp.einsum(
        "rje,rjd->jed", gelu_blocks, cot_blocks, preferred_element_type=jnp.float32
    )
    gelu_grad = jnp.einsum(
        "rjd,jed->rje", cot_blocks, contract_weight, preferred_element_type=jnp.float32
    )
    upstream = gelu_back(gelu_grad.reshape(tok_rows, hidden_count, block_size))[0].astype(
        jnp.bfloat16
    )
    section_terms = [None] * sections
    for section in reversed(range(sections)):
        section_term = jnp.einsum(
            "rlsc,rld->lscd", saved[section], upstream, preferred_element_type=jnp.float32
        )
        local_part = jnp.einsum(
            "rld,lcd->rlc",
            upstream,
            section_weight[section, :, 0],
            preferred_element_type=jnp.float32,
        )
        outgoing = jnp.einsum(
            "rld,lcd->rlc",
            upstream,
            section_weight[section, :, 1],
            preferred_element_type=jnp.float32,
        ).astype(jnp.bfloat16)
        arrived = from_partner(outgoing, "mp", section)
        inverse = jnp.argsort(pattern[section])
        upstream = jnp.take(local_part + arrived.astype(jnp.float32), inverse, axis=1).astype(
            jnp.bfloat16
        )
        section_terms[section] = section_term
    first_grad = upstream.reshape(tok_rows, feat_blocks, hidden_width)
    expand_term = jnp.einsum(
        "rmi,rmo->mio", tok_blocks, first_grad, preferred_element_type=jnp.float32
    )
    input_grad = jnp.einsum(
        "rmo,mio->rmi", first_grad, expand_weight, preferred_element_type=jnp.float32
    )
    input_grad = input_grad.reshape(tok_rows, feat_blocks * block_size).astype(jnp.bfloat16)
    summed = (
        lax.psum_scatter(
            jnp.stack(section_terms).astype(jnp.bfloat16), "dp", scatter_dimension=3, tiled=True
        ).astype(jnp.float32),
        lax.psum_scatter(
            expand_term.astype(jnp.bfloat16), "dp", scatter_dimension=1, tiled=True
        ).astype(jnp.float32),
        lax.psum_scatter(
            contract_term.astype(jnp.bfloat16), "dp", scatter_dimension=1, tiled=True
        ).astype(jnp.float32),
    )
    section_grad = (summed[0] * grad_scale).astype(jnp.bfloat16)
    expand_grad = (summed[1] * grad_scale).astype(jnp.bfloat16)
    contract_grad = (summed[2] * grad_scale).astype(jnp.bfloat16)
    return (output, input_grad, expand_grad, section_grad, contract_grad)


def solution(mesh):
    return jax.shard_map(
        body,
        mesh=mesh,
        in_specs=(
            P("dp", "mp"),
            P("mp", None, None),
            P(None, "mp", None, None, None),
            P("mp", None, None),
            P(),
            P("dp", "mp"),
        ),
        out_specs=(
            P("dp", "mp"),
            P("dp", "mp"),
            P("mp", "dp", None),
            P(None, "mp", None, "dp", None),
            P("mp", "dp", None),
        ),
        check_vma=False,
    )
```

profile of v0, /device:TPU:1, one launch (start us, length us, event | category | flops | bytes accessed | tf_op | source)
XLA Modules:
  0.0 504.2 jit_solution(17821123786561612487)
XLA Ops:
  7.2 1.9 convolution_convert_fusion.2
  10.1 3.3 collective-permute-start
  13.9 1.3 copy.79
  15.2 1.0 sort.59
  16.2 1.0 sort.60
  17.1 1.0 sort.61
  18.1 1.0 sort.62
  19.1 2.3 fusion.18
  22.2 5.6 %fusion.101 = (bf16[1,8,2,256,256]{4,3,2,1,0:T(8,128)(2,1)S(1)}, bf16[1,8,2,256,256]{4,3,2,1,0:T(8,128)(2,1)}, bf16[1,8,2,256,256]{4,3,2,1,0:T(8,128)(2,1)}) fusion(bf16[4,8,2,256,256]{4,3,2,1,0:T(8,128)(2,1)} %param.12), kind=kLoop, calls=%fused_computation.170 | loop fusion | bytes 12582912 | tf_op jit(solution)/shard_map/slice | solution.py:38
  27.8 7.9 %collective-permute-done.1 = bf16[128,8,256]{2,0,1:T(8,128)(2,1)S(1)} collective-permute-done((bf16[128,8,256]{2,0,1:T(8,128)(2,1)S(1)}, bf16[128,8,256]{2,0,1:T(8,128)(2,1)S(1)}, u32[]{:S(2)}, u32[]{:S(2)}) %collective-permute-start.1) | collective-permute-done | bytes 524320 | tf_op jit(solution)/shard_map/ppermute | solution.py:10
  38.0 12.6 %collective-permute-done.2 = bf16[128,8,256]{2,0,1:T(8,128)(2,1)S(1)} collective-permute-done((bf16[128,8,256]{2,0,1:T(8,128)(2,1)S(1)}, bf16[128,8,256]{2,0,1:T(8,128)(2,1)S(1)}, u32[]{:S(2)}, u32[]{:S(2)}) %collective-permute-start.2) | collective-permute-done | bytes 524320 | tf_op jit(solution)/shard_map/ppermute | solution.py:10
  51.3 2.1 fusion.22
  54.2 1.5 collective-permute-start.3
  55.7 11.8 %collective-permute-done.3 = bf16[128,8,256]{2,0,1:T(8,128)(2,1)S(1)} collective-permute-done((bf16[128,8,256]{2,0,1:T(8,128)(2,1)S(1)}, bf16[128,8,256]{2,0,1:T(8,128)(2,1)S(1)}, u32[]{:S(2)}, u32[]{:S(2)}) %collective-permute-start.3) | collective-permute-done | bytes 524320 | tf_op jit(solution)/shard_map/ppermute | solution.py:10
  67.5 5.7 %fusion.48 = (bf16[128,8,256]{2,0,1:T(8,128)(2,1)S(1)}, f32[128,8,256]{2,0,1:T(8,128)}, f32[8,128,256]{2,1,0:T(8,128)}) fusion(f32[128,8,256]{2,0,1:T(8,128)S(1)} %copy-done.19, bf16[1,8,2,256,256]{4,3,2,1,0:T(8,128)(2,1)} %get-tuple-element.41, bf16[128,8,1,256]{3,0,1,2:T(8,128)(2,1)S(1)} %bitcast.348, bf16[128,8,1,256]{3,0,1,2:T(8,128)(2,1)S(1)} %get-tuple-element.43), kind=kOutput, calls=%fused_computation.86 | convolution fusion | flops 287834112 | bytes 6815744 | tf_op jit(solution)/shard_map/rlsc,lscd->rld/dot_general | solution.py:37
  73.3 1.9 fusion.23
  75.2 1.6 collective-permute-start.4
  76.8 10.8 %collective-permute-done.4 = bf16[128,8,256]{2,0,1:T(8,128)(2,1)S(1)} collective-permute-done((bf16[128,8,256]{2,0,1:T(8,128)(2,1)S(1)}, bf16[128,8,256]{2,0,1:T(8,128)(2,1)S(1)}, u32[]{:S(2)}, u32[]{:S(2)}) %collective-permute-start.4) | collective-permute-done | bytes 524320 | tf_op jit(solution)/shard_map/ppermute | solution.py:10
  87.6 1.7 convert_add_fusion.3
  89.9 1.9 fusion.24
  91.8 1.0 collective-permute-start.5
  92.8 8.9 %collective-permute-done.5 = bf16[128,8,256]{2,0,1:T(8,128)(2,1)S(1)} collective-permute-done((bf16[128,8,256]{2,0,1:T(8,128)(2,1)S(1)}, bf16[128,8,256]{2,0,1:T(8,128)(2,1)S(1)}, u32[]{:S(2)}, u32[]{:S(2)}) %collective-permute-start.5) | collective-permute-done | bytes 524320 | tf_op jit(solution)/shard_map/ppermute | solution.py:10
  101.7 2.5 convert_add_fusion.2
  104.3 1.7 gather_fusion.5
  106.0 2.8 fusion.25
  109.9 1.4 convolution_convert_fusion
  111.4 2.2 convert_bitcast_fusion
  113.6 4.5 collective-permute-done.6
  118.0 2.7 convert_add_fusion.1
  120.7 2.4 gather_fusion.6
  123.1 2.0 fusion.26
  125.1 5.5 %collective-permute-start.7 = (bf16[128,8,256]{2,0,1:T(8,128)(2,1)S(1)}, bf16[128,8,256]{2,0,1:T(8,128)(2,1)S(1)}, u32[]{:S(2)}, u32[]{:S(2)}) collective-permute-start(bf16[128,8,256]{2,0,1:T(8,128)(2,1)S(1)} %fusion.26), channel_id=1, source_target_pairs={{0,1},{1,0},{2,3},{3,2},{4,5},{5,4},{6,7},{7,6},{8,9},{9,8},{10,11... | collective-permute-start | bytes 1572872 | tf_op jit(solution)/shard_map/ppermute | solution.py:10
  130.6 2.2 convert_bitcast_fusion.1
  132.8 2.1 convert_bitcast_fusion.2
  134.9 3.2 convert_bitcast_fusion.3
  138.1 2.5 convert_add_fusion
  140.7 2.5 gather_fusion.7
  143.1 2.1 bitcast_convert_fusion
  145.2 2.1 copy.89
  147.3 2.4 fusion.6
  149.7 3.7 copy.93
  153.5 6.7 %pad_maximum_fusion = bf16[4,8,2,256,256]{4,3,2,1,0:T(8,128)(2,1)} fusion(bf16[1,8,2,256,256]{4,3,2,1,0:T(8,128)(2,1)S(1)} %convert_bitcast_fusion, bf16[1,8,2,256,256]{4,3,2,1,0:T(8,128)(2,1)} %convert_bitcast_fusion.1, bf16[1,8,2,256,256]{4,3,2,1,0:T(8,128)(2,1)} %convert_bitcast_fusion.2, bf16[1,8,2,256,256]{4,3,2,1,0:T(8,128)(2,1)} %convert_bitcast_fusion.3), kind=kLoop, calls=%fused_computation.8 | loop fusion | flops 12582912 | bytes 16777216 | tf_op jit(solution)/shard_map/stack | solution.py:92
  164.7 36.7 %reduce-scatter.5.cloned.1.call-done = bf16[2,64,256]{2,1,0:T(8,128)(2,1)} async-done(((bf16[2,1024,256]{2,1,0:T(8,128)(2,1)}), bf16[2,64,256]{2,1,0:T(8,128)(2,1)}) %reduce-scatter.5.cloned.1.call-update) | async-done | bytes 65552 | tf_op jit(solution)/shard_map/reduce_scatter | solution.py:97
  201.4 1.5 multiply_convert_fusion.1
  202.9 160.0 %all-reduce.3.cloned.1.call-done = bf16[2,256,1024]{2,0,1:T(2,128)(2,1)} async-done(((bf16[2,256,1024]{2,0,1:T(2,128)(2,1)}), bf16[2,256,1024]{2,0,1:T(2,128)(2,1)}) %all-reduce.3.cloned.1.call-update) | async-done | bytes 1048592
  362.8 0.9 multiply_convert_fusion.2
  364.4 131.3 %reduce-scatter.3.cloned.1.call-done = bf16[4,8,2,16,256]{4,3,2,1,0:T(8,128)(2,1)} async-done(((bf16[4,8,2,256,256]{4,3,2,1,0:T(8,128)(2,1)}), bf16[4,8,2,16,256]{4,3,2,1,0:T(8,128)(2,1)}) %reduce-scatter.3.cloned.1.call-update) | async-done | bytes 524304 | tf_op jit(solution)/shard_map/reduce_scatter | solution.py:91
  495.7 2.0 multiply_convert_fusion
  (117 shorter events, 12.4 us)
Async XLA Ops:
  7.2 6.3 %copy-start = (bf16[2,1024,256]{2,1,0:T(8,128)(2,1)S(1)}, bf16[2,1024,256]{2,1,0:T(8,128)(2,1)}, u32[]{:S(2)}) copy-start(bf16[2,1024,256]{2,1,0:T(8,128)(2,1)} %param.13) | copy-start | bytes 3145732
  7.2 2.1 copy-start.29
  7.2 194.2 %reduce-scatter.5.cloned.1.call-start = ((), (), s32[]{:S(2)}) async-start(), calls=%async_computation.3 | async-start | bytes 1114112 | tf_op jit(solution)/shard_map/reduce_scatter | solution.py:97
  9.1 4.4 copy-start.27
  10.1 9.0 %copy-start.7 = (bf16[128,8,1,256]{3,0,2,1:T(8,128)(2,1)}, bf16[128,8,1,256]{3,0,2,1:T(8,128)(2,1)S(1)}, u32[]{:S(2)}) copy-start(bf16[128,8,1,256]{3,0,2,1:T(8,128)(2,1)S(1)} %get-tuple-element.49) | copy-start | bytes 1572868
  10.1 9.0 %collective-permute-start = (bf16[128,8,256]{2,0,1:T(8,128)(2,1)S(1)}, bf16[128,8,256]{2,0,1:T(8,128)(2,1)}, u32[]{:S(2)}, u32[]{:S(2)}) collective-permute-start(bf16[128,8,256]{2,0,1:T(8,128)(2,1)S(1)} %get-tuple-element.50), channel_id=1, source_target_pairs={{0,1},{1,0},{2,3},{3,2},{4,5},{5,4},{6,7},{7,6},{8,9},{9,8},{10,11... | collective-permute-start | bytes 1572872 | tf_op jit(solution)/shard_map/ppermute | solution.py:10
  22.1 13.6 %copy-start.9 = (bf16[128,8,1,256]{3,0,1,2:T(8,128)(2,1)}, bf16[128,8,1,256]{3,0,1,2:T(8,128)(2,1)S(1)}, u32[]{:S(2)}) copy-start(bf16[128,8,1,256]{3,0,1,2:T(8,128)(2,1)S(1)} %get-tuple-element.47) | copy-start | bytes 1572868
  22.1 13.6 %collective-permute-start.1 = (bf16[128,8,256]{2,0,1:T(8,128)(2,1)S(1)}, bf16[128,8,256]{2,0,1:T(8,128)(2,1)S(1)}, u32[]{:S(2)}, u32[]{:S(2)}) collective-permute-start(bf16[128,8,256]{2,0,1:T(8,128)(2,1)S(1)} %get-tuple-element.48), channel_id=1, source_target_pairs={{0,2},{1,3},{2,0},{3,1},{4,6},{5,7},{6,4},{7,5},{8,10},{9,11},{10,... | collective-permute-start | bytes 1572872 | tf_op jit(solution)/shard_map/ppermute | solution.py:10
  35.8 0.8 copy-start.23
  37.8 12.7 %copy-start.11 = (bf16[128,8,1,256]{3,0,1,2:T(8,128)(2,1)}, bf16[128,8,1,256]{3,0,1,2:T(8,128)(2,1)S(1)}, u32[]{:S(2)}) copy-start(bf16[128,8,1,256]{3,0,1,2:T(8,128)(2,1)S(1)} %get-tuple-element.45) | copy-start | bytes 1572868
  37.8 12.7 %collective-permute-start.2 = (bf16[128,8,256]{2,0,1:T(8,128)(2,1)S(1)}, bf16[128,8,256]{2,0,1:T(8,128)(2,1)S(1)}, u32[]{:S(2)}, u32[]{:S(2)}) collective-permute-start(bf16[128,8,256]{2,0,1:T(8,128)(2,1)S(1)} %get-tuple-element.46), channel_id=1, source_target_pairs={{0,4},{1,5},{2,6},{3,7},{4,0},{5,1},{6,2},{7,3},{8,12},{9,13},{10,... | collective-permute-start | bytes 1572872 | tf_op jit(solution)/shard_map/ppermute | solution.py:10
  50.6 0.8 copy-start.25
  53.5 14.1 %copy-start.19 = (f32[128,8,256]{2,0,1:T(8,128)S(1)}, f32[128,8,256]{2,0,1:T(8,128)}, u32[]{:S(2)}) copy-start(f32[128,8,256]{2,0,1:T(8,128)} %copy.79) | copy-start | bytes 3145732
  54.2 19.1 %copy-start.6 = (bf16[128,8,1,256]{3,0,1,2:T(8,128)(2,1)}, bf16[128,8,1,256]{3,0,1,2:T(8,128)(2,1)S(1)}, u32[]{:S(2)}) copy-start(bf16[128,8,1,256]{3,0,1,2:T(8,128)(2,1)S(1)} %get-tuple-element.43) | copy-start | bytes 1572868
  54.2 13.3 %collective-permute-start.3 = (bf16[128,8,256]{2,0,1:T(8,128)(2,1)S(1)}, bf16[128,8,256]{2,0,1:T(8,128)(2,1)S(1)}, u32[]{:S(2)}, u32[]{:S(2)}) collective-permute-start(bf16[128,8,256]{2,0,1:T(8,128)(2,1)S(1)} %get-tuple-element.44), channel_id=1, source_target_pairs={{0,8},{1,9},{2,10},{3,11},{4,12},{5,13},{6,14},{7,15},{8,0},{9,1},... | collective-permute-start | bytes 1572872 | tf_op jit(solution)/shard_map/ppermute | solution.py:10
  67.5 5.7 %copy-start.22 = (bf16[128,8,256]{2,0,1:T(8,128)(2,1)}, bf16[128,8,256]{2,0,1:T(8,128)(2,1)S(1)}, u32[]{:S(2)}) copy-start(bf16[128,8,256]{2,0,1:T(8,128)(2,1)S(1)} %collective-permute-done.3) | copy-start | bytes 1572868
  73.3 14.3 %copy-start.1 = (bf16[128,8,256]{2,0,1:T(8,128)(2,1)}, bf16[128,8,256]{2,0,1:T(8,128)(2,1)S(1)}, u32[]{:S(2)}) copy-start(bf16[128,8,256]{2,0,1:T(8,128)(2,1)S(1)} %get-tuple-element.30) | copy-start | bytes 1572868
  75.2 12.4 %collective-permute-start.4 = (bf16[128,8,256]{2,0,1:T(8,128)(2,1)S(1)}, bf16[128,8,256]{2,0,1:T(8,128)(2,1)S(1)}, u32[]{:S(2)}, u32[]{:S(2)}) collective-permute-start(bf16[128,8,256]{2,0,1:T(8,128)(2,1)S(1)} %fusion.23), channel_id=1, source_target_pairs={{0,8},{1,9},{2,10},{3,11},{4,12},{5,13},{6,14},{7,15},{8,0},{9,1},... | collective-permute-start | bytes 1572872 | tf_op jit(solution)/shard_map/ppermute | solution.py:10
  89.9 14.4 %copy-start.13 = (bf16[8,128,256]{2,1,0:T(8,128)(2,1)}, bf16[8,128,256]{2,1,0:T(8,128)(2,1)S(1)}, u32[]{:S(2)}) copy-start(bf16[8,128,256]{2,1,0:T(8,128)(2,1)S(1)} %gather_fusion.4) | copy-start | bytes 1572868
  91.8 10.0 %collective-permute-start.5 = (bf16[128,8,256]{2,0,1:T(8,128)(2,1)S(1)}, bf16[128,8,256]{2,0,1:T(8,128)(2,1)S(1)}, u32[]{:S(2)}, u32[]{:S(2)}) collective-permute-start(bf16[128,8,256]{2,0,1:T(8,128)(2,1)S(1)} %fusion.24), channel_id=1, source_target_pairs={{0,4},{1,5},{2,6},{3,7},{4,0},{5,1},{6,2},{7,3},{8,12},{9,13},{10,... | collective-permute-start | bytes 1572872 | tf_op jit(solution)/shard_map/ppermute | solution.py:10
  104.3 5.2 %copy-start.20 = (f32[128,8,256]{2,0,1:T(8,128)S(1)}, f32[128,8,256]{2,0,1:T(8,128)}, u32[]{:S(2)}) copy-start(f32[128,8,256]{2,0,1:T(8,128)} %get-tuple-element.31) | copy-start | bytes 3145732
  106.0 3.4 copy-start.15
  106.0 3.4 copy-start.21
  108.7 9.3 %collective-permute-start.6 = (bf16[128,8,256]{2,0,1:T(8,128)(2,1)}, bf16[128,8,256]{2,0,1:T(8,128)(2,1)}, u32[]{:S(2)}, u32[]{:S(2)}) collective-permute-start(bf16[128,8,256]{2,0,1:T(8,128)(2,1)} %fusion.25), channel_id=1, source_target_pairs={{0,2},{1,3},{2,0},{3,1},{4,6},{5,7},{6,4},{7,5},{8,10},{9,11},{10,... | collective-permute-start | bytes 1572872 | tf_op jit(solution)/shard_map/ppermute | solution.py:10
  109.9 1.4 copy-start.2
  111.3 251.5 %all-reduce.3.cloned.1.call-start = ((), (), s32[]{:S(2)}) async-start(), calls=%async_computation.4 | async-start | bytes 2097152
  111.4 6.6 %copy-start.16 = (bf16[8,128,256]{2,1,0:T(8,128)(2,1)S(1)}, bf16[8,128,256]{2,1,0:T(8,128)(2,1)}, u32[]{:S(2)}) copy-start(bf16[8,128,256]{2,1,0:T(8,128)(2,1)} %copy-done.15) | copy-start | bytes 1572868
  123.1 7.5 %copy-start.12 = (bf16[128,8,1,256]{3,0,1,2:T(8,128)(2,1)S(1)}, bf16[128,8,1,256]{3,0,1,2:T(8,128)(2,1)}, u32[]{:S(2)}) copy-start(bf16[128,8,1,256]{3,0,1,2:T(8,128)(2,1)} %copy-done.11) | copy-start | bytes 1572868
  123.1 7.5 %copy-start.14 = (bf16[8,128,256]{2,1,0:T(8,128)(2,1)S(1)}, bf16[8,128,256]{2,1,0:T(8,128)(2,1)}, u32[]{:S(2)}) copy-start(bf16[8,128,256]{2,1,0:T(8,128)(2,1)} %copy-done.13) | copy-start | bytes 1572868
  123.1 7.5 %copy-start.26 = (bf16[128,8,256]{2,0,1:T(8,128)(2,1)S(1)}, bf16[128,8,256]{2,0,1:T(8,128)(2,1)}, u32[]{:S(2)}) copy-start(bf16[128,8,256]{2,0,1:T(8,128)(2,1)} %copy-done.25) | copy-start | bytes 1572868
  125.1 7.7 %copy-start.10 = (bf16[128,8,1,256]{3,0,1,2:T(8,128)(2,1)S(1)}, bf16[128,8,1,256]{3,0,1,2:T(8,128)(2,1)}, u32[]{:S(2)}) copy-start(bf16[128,8,1,256]{3,0,1,2:T(8,128)(2,1)} %copy-done.9) | copy-start | bytes 1572868
  125.1 7.7 %copy-start.17 = (bf16[8,128,256]{2,1,0:T(8,128)(2,1)S(1)}, bf16[8,128,256]{2,1,0:T(8,128)(2,1)}, u32[]{:S(2)}) copy-start(bf16[8,128,256]{2,1,0:T(8,128)(2,1)} %copy-done.15) | copy-start | bytes 1572868
  125.1 7.7 %copy-start.24 = (bf16[128,8,256]{2,0,1:T(8,128)(2,1)S(1)}, bf16[128,8,256]{2,0,1:T(8,128)(2,1)}, u32[]{:S(2)}) copy-start(bf16[128,8,256]{2,0,1:T(8,128)(2,1)} %copy-done.23) | copy-start | bytes 1572868
  125.1 13.0 %collective-permute-start.7 = (bf16[128,8,256]{2,0,1:T(8,128)(2,1)S(1)}, bf16[128,8,256]{2,0,1:T(8,128)(2,1)S(1)}, u32[]{:S(2)}, u32[]{:S(2)}) collective-permute-start(bf16[128,8,256]{2,0,1:T(8,128)(2,1)S(1)} %fusion.26), channel_id=1, source_target_pairs={{0,1},{1,0},{2,3},{3,2},{4,5},{5,4},{6,7},{7,6},{8,9},{9,8},{10,11... | collective-permute-start | bytes 1572872 | tf_op jit(solution)/shard_map/ppermute | solution.py:10
  132.8 2.1 copy-start.8
  132.8 2.1 copy-start.18
  140.7 6.6 %copy-start.28 = (bf16[128,512]{1,0:T(8,128)(2,1)S(1)}, bf16[128,512]{1,0:T(8,128)(2,1)}, u32[]{:S(2)}) copy-start(bf16[128,512]{1,0:T(8,128)(2,1)} %param.10) | copy-start | bytes 393220
  153.4 342.3 %reduce-scatter.3.cloned.1.call-start = ((), (), s32[]{:S(2)}) async-start(), calls=%async_computation.2 | async-start | bytes 8912896 | tf_op jit(solution)/shard_map/reduce_scatter | solution.py:91
  160.2 0.7 copy-start.30
  160.2 1.9 copy-start.3
  160.2 3.2 copy-start.4
  160.2 3.1 copy-start.5
Sparse Core Ops, SparseCore 0:
  111.4 89.9 reduce-scatter.4
  204.2 158.5 all-reduce.2
  366.6 129.1 reduce-scatter.2
where the time goes:
time: 505 us; the launch traced here: 504 us
  waiting for transfers between devices  384 us (76%)
  matrix products  45.1 us (9%)
  local copies, waits for them, and re-layouts  28.1 us (6%)
  other arithmetic  17.8 us (4%)
  between operations  14.9 us (3%)
  starting transfers between devices  13.9 us (3%)
    unnamed x4, waiting for transfers between devices  160 us
    reduce_scatter x1, waiting for transfers between devices, body(): lax.psum_scatter(jnp.stack(section_terms).astype(jnp.bfloat16), 'dp', sca...  131 us
    ppermute x8, waiting for transfers between devices, from_partner(): lax.ppermute(shard, axis, [(i, i ^ 1 << apart) for i in range(lax.axis_si...  56.5 us
    reduce_scatter x1, waiting for transfers between devices, body(): lax.psum_scatter(contract_term.astype(jnp.bfloat16), 'dp', scatter_dimens...  36.7 us
    ppermute x8, starting transfers between devices, from_partner(): lax.ppermute(shard, axis, [(i, i ^ 1 << apart) for i in range(lax.axis_si...  13.7 us
    dot_general x4, matrix products, body(): jnp.einsum('rlsc,lscd->rld', paired, section_weight[section], preferred_e...  10.6 us
  transfers between devices with their start and end apart: 11, of which 9 were waited for; matrix products, arithmetic and copies ran while one was open for 12% of the time, Pallas kernels for 0%

commit v1 on v0

v1 whole, which is shorter than its diff:
```python
import math

import jax
import jax.numpy as jnp
from jax import lax
from jax.experimental import pallas as pl
from jax.experimental.pallas import tpu as pltpu
from jax.sharding import PartitionSpec as P

MESH = pl.DeviceIdType.MESH
BF16, F32 = jnp.bfloat16, jnp.float32
BLK = 256
ROWS = 128
CHUNKS = 2
PIECE = ROWS // CHUNKS
SECTIONS = 4
HIDDEN = 8
HALF = 4
SHARDS = 16
COPIES = 96


def dot(left, right, left_dim, right_dim):
    return lax.dot_general(
        left, right, (((left_dim,), (right_dim,)), ((), ())), preferred_element_type=F32
    )


def each(count, unroll, step):
    def several(at, carry):
        for more in range(unroll):
            step(at * unroll + more)
        return carry

    lax.fori_loop(0, count // unroll, several, 0)


def kernel(
    scale, pattern, tokens_hbm, expand_hbm, section_hbm, contract_hbm, cot_hbm,
    out_hbm, in_grad_hbm, expand_grad_hbm, section_grad_hbm, contract_grad_hbm,
    tok, cot, expand_w, section_w, contract_w, chosen, paired, grads, act, hidden, total, gelu_grad,
    u_out, u_in, part_s, part_c, part_e, r1_s, r1_c, r1_e, r2_s, r2_c, r2_e, r3_s, r3_c, r3_e,
    fin_s, fin_c, fin_e, far_s, far_c, far_e, out_v, in_grad_v,
    send_sem, recv_sem, local_sem,
):
    dp, mp = lax.axis_index("dp"), lax.axis_index("mp")
    core = mp % 2
    zh, y = dp // 4, dp % 4
    near_y, cross_y = y + 1 - 2 * (y % 2), 3 - y
    near_z, cross_z = zh + 1 - 2 * (zh % 2), 3 - zh
    ya = near_y + core * (cross_y - near_y)
    yb = cross_y + core * (near_y - cross_y)
    za = near_z + core * (cross_z - near_z)
    zb = cross_z + core * (near_z - cross_z)
    to_ya, to_yb = (zh * 4 + ya, mp), (zh * 4 + yb, mp)
    to_za, to_zb = (za * 4 + y, mp), (zb * 4 + y, mp)
    across = [
        (dp, mp + 2**k - 2 * 2**k * ((mp // 2**k) % 2)) for k in range(SECTIONS)
    ]
    half = (y + y // 2) % 2 * (1 - core) + y // 2 * core
    mine, theirs = half * HALF, (1 - half) * HALF

    def split(own, other):
        low, high = (own + other) % 2, (own // 2 + other // 2) % 2
        both = (low + high) % 2
        return both + core * (high - both), high + core * (both - high)

    slot = []
    for shard in range(SHARDS):
        z_first, z_second = split(zh, shard // 4)
        y_last, y_first = split(y, shard % 4)
        slot.append(8 * y_first + 4 * z_first + 2 * z_second + y_last)

    loads, sends = [], []

    def load(src, dst):
        copy = pltpu.make_async_copy(src, dst, local_sem.at[len(loads)])
        copy.start()
        loads.append(copy)
        return copy

    def send(src, dst, device):
        at = len(sends)
        copy = pltpu.make_async_remote_copy(
            src_ref=src,
            dst_ref=dst,
            send_sem=send_sem.at[at],
            recv_sem=recv_sem.at[at],
            device_id=device,
            device_id_type=MESH,
        )
        copy.start()
        sends.append(copy)
        return copy

    tok_in = [load(tokens_hbm.at[:, pl.ds(j * BLK, BLK)], tok.at[j, pl.ds(0, ROWS)]) for j in range(2)]
    expand_in = load(expand_hbm, expand_w)
    section_in = [load(section_hbm.at[0], section_w.at[0])]
    cot_in = [load(cot_hbm.at[:, pl.ds(j * BLK, BLK)], cot.at[j, pl.ds(0, ROWS)]) for j in range(2)]
    contract_in = load(contract_hbm, contract_w)
    section_in += [load(section_hbm.at[k], section_w.at[k]) for k in range(1, SECTIONS)]

    barrier = pltpu.get_barrier_semaphore()
    peers = [*across, to_ya, to_yb, to_za, to_zb]
    for device in peers:
        pl.semaphore_signal(barrier, inc=1, device_id=device, device_id_type=MESH)

    inverse = []
    for k in range(SECTIONS):
        row = []
        for c in range(HIDDEN):
            place = jnp.int32(0)
            for m in range(1, HIDDEN):
                place = jnp.where(pattern[k, m] == c, jnp.int32(m), place)
            row.append(place)
        inverse.append(row)

    def rows(piece):
        return pl.ds(piece * PIECE, PIECE)

    def expand(piece):
        for j in range(2):
            source = tok[j, rows(piece)]
            for i in range(4):
                hidden[j * 4 + i, rows(piece)] = dot(
                    source, expand_w[j, :, i * BLK : (i + 1) * BLK], 1, 0
                ).astype(BF16)

    def choose(k, piece):
        for m in range(HIDDEN):
            chosen[k, m, rows(piece)] = hidden[pattern[k, m], rows(piece)]

    def exchange(k, piece):
        return send(
            chosen.at[k, :, rows(piece)], paired.at[k, :, rows(piece)], across[k]
        )

    def own_part(k, piece):
        def one(b):
            total[b, rows(piece)] = dot(
                chosen[k, b, rows(piece)], section_w[k, b, 0], 1, 0
            )

        each(HIDDEN, 4, one)

    def pair_part(k, piece, use):
        def one(b):
            use(
                b,
                total[b, rows(piece)]
                + dot(paired[k, b, rows(piece)], section_w[k, b, 1], 1, 0),
            )

        each(HIDDEN, 4, one)

    def to_hidden(piece):
        def use(b, value):
            hidden[b, rows(piece)] = value.astype(BF16)

        return use

    def to_gelu(piece):
        def use(b, z):
            below = 0.5 * (1.0 + lax.erf(z * math.sqrt(0.5)))
            act[b, rows(piece)] = (z * below).astype(BF16)
            slope = below + z * (jnp.exp(-0.5 * z * z) * (1.0 / math.sqrt(2.0 * math.pi)))
            grads[SECTIONS, b, rows(piece)] = (
                gelu_grad[b, rows(piece)] * slope
            ).astype(BF16)

        return use

    def share(ref):
        part = ref.at[pl.ds(theirs, HALF)]
        return send(part.at[:, pl.ds(0, ROWS)], part.at[:, pl.ds(ROWS, ROWS)], to_ya)

    def share_feature(ref):
        part = ref.at[1 - half]
        return send(part.at[pl.ds(0, ROWS)], part.at[pl.ds(ROWS, ROWS)], to_ya)

    def back(k, piece):
        def far(b):
            u_out[k, b, rows(piece)] = dot(
                grads[k + 1, b, rows(piece)], section_w[k, b, 1], 1, 1
            ).astype(BF16)

        each(HIDDEN, 4, far)
        copy = send(u_out.at[k, :, rows(piece)], u_in.at[k, :, rows(piece)], across[k])

        def near(b):
            total[b, rows(piece)] = dot(
                grads[k + 1, b, rows(piece)], section_w[k, b, 0], 1, 1
            )

        each(HIDDEN, 4, near)
        return copy

    def gather_back(k, piece):
        def one(b):
            hidden[b, rows(piece)] = (
                total[b, rows(piece)] + u_in[k, b, rows(piece)].astype(F32)
            ).astype(BF16)

        each(HIDDEN, 4, one)
        for c in range(HIDDEN):
            grads[k, c, rows(piece)] = hidden[inverse[k][c], rows(piece)]

    class Reduction:
        def __init__(self, part, r1, r2, r3, fin, far, unroll):
            self.part, self.r1, self.r2, self.r3 = part, r1, r2, r3
            self.fin, self.far, self.unroll = fin, far, unroll

        def first(self):
            self.copy = send(self.part.at[pl.ds(8, 8)], self.r1, to_yb)

        def add(self, received, count):
            def one(at):
                self.part[at] = (
                    self.part[at].astype(F32) + received[at].astype(F32)
                ).astype(BF16)

            each(count, self.unroll, one)

        def second(self):
            self.copy.wait_recv()
            self.add(self.r1, 8)
            self.copy = send(self.part.at[pl.ds(4, 4)], self.r2, to_za)

        def third(self):
            self.copy.wait_recv()
            self.add(self.r2, 4)
            self.copy = send(self.part.at[pl.ds(2, 2)], self.r3, to_zb)

        def fourth(self, own):
            self.copy.wait_recv()
            for at in range(2):
                self.fin[at] = (
                    (self.part[at].astype(F32) + self.r3[at].astype(F32)) * scale
                ).astype(BF16)
            self.copy = send(self.fin.at[1], self.far, to_ya)
            load(self.fin.at[0], own)

        def fifth(self, other):
            self.copy.wait_recv()
            load(self.far, other)

    reduce_s = [
        Reduction(part_s.at[k], r1_s.at[k], r2_s.at[k], r3_s.at[k], fin_s.at[k], far_s.at[k], 1)
        for k in range(SECTIONS)
    ]
    reduce_c = Reduction(part_c, r1_c, r2_c, r3_c, fin_c, far_c, 2)
    reduce_e = Reduction(part_e, r1_e, r2_e, r3_e, fin_e, far_e, 2)

    def section_terms(k):
        for i in range(HALF):
            upstream = grads[k + 1, mine + i]
            for s, ref in enumerate((chosen, paired)):
                term = dot(ref[k, mine + i], upstream, 0, 0).astype(BF16)
                for shard in range(SHARDS):
                    part_s[k, slot[shard], i, s] = term[shard * 16 : (shard + 1) * 16]
        reduce_s[k].first()

    def contract_terms():
        for i in range(HALF):
            term = dot(act[mine + i], cot[half], 0, 0).astype(BF16)
            for q in range(4):
                part_c[slot[i * 4 + q]] = term[q * 64 : (q + 1) * 64]
        reduce_c.first()

    def expand_terms():
        for i in range(HALF):
            term = dot(tok[half], grads[0, mine + i], 0, 0).astype(BF16)
            for shard in range(SHARDS):
                part_e[slot[shard], :, i * BLK : (i + 1) * BLK] = term[shard * 16 : (shard + 1) * 16]
        reduce_e.first()

    pieces = range(CHUNKS)
    coming = [None] * CHUNKS
    shared = {}

    for copy in tok_in:
        copy.wait()
    expand_in.wait()
    for piece in pieces:
        expand(piece)
        choose(0, piece)
        if piece == 0:
            pl.semaphore_wait(barrier, len(peers))
        coming[piece] = exchange(0, piece)
        if piece == 0:
            section_in[0].wait()
        own_part(0, piece)
    shared["tok"] = share_feature(tok)
    shared["own", 0] = share(chosen.at[0])
    for k in range(SECTIONS - 1):
        section_in[k + 1].wait()
        for piece in pieces:
            coming[piece].wait_recv()
            pair_part(k, piece, to_hidden(piece))
            choose(k + 1, piece)
            coming[piece] = exchange(k + 1, piece)
            own_part(k + 1, piece)
        shared["pair", k] = share(paired.at[k])
        shared["own", k + 1] = share(chosen.at[k + 1])
        if k == 0:
            for copy in cot_in:
                copy.wait()
            contract_in.wait()
            shared["cot"] = share_feature(cot)

            def gelu_grads(j):
                source = cot[j, pl.ds(0, ROWS)]
                for i in range(4):
                    gelu_grad[j * 4 + i] = dot(
                        source, contract_w[j, i * BLK : (i + 1) * BLK], 1, 1
                    )

            each(2, 1, gelu_grads)

    for piece in pieces:
        coming[piece].wait_recv()
        pair_part(SECTIONS - 1, piece, to_gelu(piece))
        coming[piece] = back(SECTIONS - 1, piece)
    shared["grad", SECTIONS] = share(grads.at[SECTIONS])
    shared["act"] = share(act)
    shared["pair", SECTIONS - 1] = share(paired.at[SECTIONS - 1])

    def outputs(j):
        sums = sum(
            dot(act[j * 4 + i, pl.ds(0, ROWS)], contract_w[j, i * BLK : (i + 1) * BLK], 1, 0)
            for i in range(4)
        )
        out_v[j] = sums.astype(BF16)

    each(2, 1, outputs)
    for j in range(2):
        load(out_v.at[j], out_hbm.at[:, pl.ds(j * BLK, BLK)])

    def await_shared(*names):
        for name in names:
            shared[name].wait_recv()

    def section_first(k):
        await_shared(("grad", k + 1), ("own", k), ("pair", k))
        section_terms(k)

    def stage(k):
        for piece in pieces:
            coming[piece].wait_recv()
            gather_back(k, piece)
            if k:
                coming[piece] = back(k - 1, piece)
        shared["grad", k] = share(grads.at[k])

    def own_grad(k):
        return section_grad_hbm.at[k, pl.ds(mine, HALF)]

    def far_grad(k):
        return section_grad_hbm.at[k, pl.ds(theirs, HALF)]

    stage(3)
    await_shared("act", "cot")
    contract_terms()
    section_first(3)
    stage(2)
    reduce_c.second()
    section_first(2)
    reduce_s[3].second()
    stage(1)
    stage(0)
    reduce_c.third()
    reduce_s[3].third()
    section_first(1)
    reduce_s[2].second()
    section_first(0)
    await_shared("tok")
    await_shared(("grad", 0))
    expand_terms()
    for j in range(2):
        sums = sum(
            dot(grads[0, j * 4 + i, pl.ds(0, ROWS)], expand_w[j, :, i * BLK : (i + 1) * BLK], 1, 1)
            for i in range(4)
        )
        in_grad_v[j] = sums.astype(BF16)
        load(in_grad_v.at[j], in_grad_hbm.at[:, pl.ds(j * BLK, BLK)])
    reduce_s[2].third()
    reduce_c.fourth(contract_grad_hbm.at[half])
    reduce_s[3].fourth(own_grad(3))
    reduce_s[1].second()
    reduce_s[0].second()
    reduce_e.second()
    reduce_s[2].fourth(own_grad(2))
    reduce_s[1].third()
    reduce_s[0].third()
    reduce_e.third()
    reduce_c.fifth(contract_grad_hbm.at[1 - half])
    reduce_s[3].fifth(far_grad(3))
    reduce_s[1].fourth(own_grad(1))
    reduce_s[0].fourth(own_grad(0))
    reduce_e.fourth(expand_grad_hbm.at[half])
    reduce_s[2].fifth(far_grad(2))
    reduce_s[1].fifth(far_grad(1))
    reduce_s[0].fifth(far_grad(0))
    reduce_e.fifth(expand_grad_hbm.at[1 - half])
    for copy in sends:
        copy.wait_send()
    for copy in loads[len(tok_in) + len(cot_in) + 2 + SECTIONS :]:
        copy.wait()


def body(tokens, expand_weight, section_weight, contract_weight, pattern, cotangent):
    scale = 1.0 / math.sqrt(tokens.shape[0] * lax.axis_size("dp"))
    hbm = pl.BlockSpec(memory_space=pl.ANY)

    def vmem(*shape, dtype=BF16):
        return pltpu.VMEM(shape, dtype)

    sec, con, exp = (HALF, 2, 16, BLK), (64, BLK), (16, 4 * BLK)
    scratch = [
        vmem(2, 2 * ROWS, BLK),
        vmem(2, 2 * ROWS, BLK),
        vmem(2, BLK, 4 * BLK),
        vmem(SECTIONS, HIDDEN, 2, BLK, BLK),
        vmem(2, 4 * BLK, BLK),
        vmem(SECTIONS, HIDDEN, 2 * ROWS, BLK),
        vmem(SECTIONS, HIDDEN, 2 * ROWS, BLK),
        vmem(SECTIONS + 1, HIDDEN, 2 * ROWS, BLK),
        vmem(HIDDEN, 2 * ROWS, BLK),
        vmem(HIDDEN, ROWS, BLK),
        vmem(HIDDEN, ROWS, BLK, dtype=F32),
        vmem(HIDDEN, ROWS, BLK, dtype=F32),
        vmem(SECTIONS, HIDDEN, ROWS, BLK),
        vmem(SECTIONS, HIDDEN, ROWS, BLK),
    ]
    for count in (16, 8, 4, 2, 2, 1):
        lead = (count,) if count > 1 else ()
        scratch += [vmem(SECTIONS, *lead, *sec), vmem(*lead, *con), vmem(*lead, *exp)]
    scratch += [vmem(2, ROWS, BLK), vmem(2, ROWS, BLK)]
    scratch += [
        pltpu.SemaphoreType.DMA((COPIES,)),
        pltpu.SemaphoreType.DMA((COPIES,)),
        pltpu.SemaphoreType.DMA((COPIES,)),
    ]
    return pl.pallas_call(
        lambda *refs: kernel(scale, *refs),
        out_shape=(
            jax.ShapeDtypeStruct((ROWS, 2 * BLK), BF16),
            jax.ShapeDtypeStruct((ROWS, 2 * BLK), BF16),
            jax.ShapeDtypeStruct((2, 16, 4 * BLK), BF16),
            jax.ShapeDtypeStruct((SECTIONS, HIDDEN, 2, 16, BLK), BF16),
            jax.ShapeDtypeStruct((2, 64, BLK), BF16),
        ),
        in_specs=[pl.BlockSpec(memory_space=pltpu.SMEM)] + [hbm] * 5,
        out_specs=(hbm,) * 5,
        scratch_shapes=scratch,
        compiler_params=pltpu.CompilerParams(
            collective_id=0, has_side_effects=True, vmem_limit_bytes=58 * 2**20
        ),
        name="butterfly",
    )(pattern, tokens, expand_weight, section_weight, contract_weight, cotangent)


def solution(mesh):
    return jax.shard_map(
        body,
        mesh=mesh,
        in_specs=(
            P("dp", "mp"),
            P("mp", None, None),
            P(None, "mp", None, None, None),
            P("mp", None, None),
            P(),
            P("dp", "mp"),
        ),
        out_specs=(
            P("dp", "mp"),
            P("dp", "mp"),
            P("mp", "dp", None),
            P(None, "mp", None, "dp", None),
            P("mp", "dp", None),
        ),
        check_vma=False,
    )
```

time: 505 us -> 136 us (0.27)
  waiting for transfers between devices: 384 us -> 0 us
  Pallas kernels: 0 us -> 127 us
  matrix products: 45.1 us -> 0 us
  local copies, waits for them, and re-layouts: 28.1 us -> 7.95 us
  other arithmetic: 17.8 us -> 0 us
  between operations: 14.9 us -> 0.64 us
  starting transfers between devices: 13.9 us -> 0 us
    reduce_scatter x2 -> x0, waiting for transfers between devices: 168 us -> none  [the longest x1 131 us: body(): lax.psum_scatter(jnp.stack(section_terms).astype(jnp.bfloat16), 'dp', sca...]
    unnamed x4 -> x0, waiting for transfers between devices: 160 us -> none
    pallas_call x0 -> x1, Pallas kernels: none -> 127 us  [body(): pl.pallas_call(lambda *refs: kernel(scale, *refs), out_shape=(jax.ShapeDt...]
    ppermute x8 -> x0, waiting for transfers between devices: 56.5 us -> none  [from_partner(): lax.ppermute(shard, axis, [(i, i ^ 1 << apart) for i in range(lax.axis_si...]
    dot_general x22 -> x0, matrix products: 45.1 us -> none  [the longest x4 10.6 us: body(): jnp.einsum('rlsc,lscd->rld', paired, section_weight[section], preferred_e...]
    ppermute x8 -> x0, starting transfers between devices: 13.7 us -> none  [from_partner(): lax.ppermute(shard, axis, [(i, i ^ 1 << apart) for i in range(lax.axis_si...]
    gather x8 -> x0, local copies, waits for them, and re-layouts: 9.52 us -> none  [the longest x4 7.2 us: body(): jnp.take(local_part + arrived.astype(jnp.float32), inverse, axis=1)]
    another operation x5 -> x0, other arithmetic: 7.23 us -> none  [the longest x1 6.67 us: body(): jnp.stack(section_terms).astype(jnp.bfloat16)]
  transfers between devices with their start and end apart: 11 -> 0, of which waited for: 9 -> 0; matrix products, arithmetic and copies ran while one was open for 12% -> 0% of each run, Pallas kernels for 0% -> 0%
where the time goes in v1:
time: 136 us
  Pallas kernels  127 us (93%)
  local copies, waits for them, and re-layouts  7.95 us (6%)
    pallas_call x1, Pallas kernels, body(): pl.pallas_call(lambda *refs: kernel(scale, *refs), out_shape=(jax.ShapeDt...  127 us
    unnamed x5, local copies, waits for them, and re-layouts  7.95 us

profile of v1, /device:TPU:1, one launch (start us, length us, event | category | flops | bytes accessed | tf_op | source)
XLA Modules:
  0.0 135.6 jit_solution(11925537304429630086)
XLA Ops:
  0.6 127.0 %butterfly.1 = (bf16[128,512]{1,0:T(8,128)(2,1)}, bf16[128,512]{1,0:T(8,128)(2,1)}, bf16[2,16,1024]{2,1,0:T(8,128)(2,1)}, bf16[4,8,2,16,256]{4,3,2,1,0:T(8,128)(2,1)}, bf16[2,64,256]{2,1,0:T(8,128)(2,1)}) custom-call(s32[4,8]{1,0:T(4,128)} %refs_0_.1, bf16[128,512]{1,0:T(8,128)(2,1)} %refs_1_.1, bf16[2,256,1024]{2,1,0:T(8,128)(2,1)} %refs_2_.1, ...), custom_call_target="tpu_custom_call" | custom-call | tf_op jit(solution)/shard_map/butterfly/pallas_call | solution.py:444
  127.6 1.6 %copy.16 = bf16[128,512]{1,0:T(8,128)(2,1)} copy(bf16[128,512]{1,0:T(8,128)(2,1)} %get-tuple-element.10) | data formatting | bytes 262144
  129.2 1.6 %copy.17 = bf16[128,512]{1,0:T(8,128)(2,1)} copy(bf16[128,512]{1,0:T(8,128)(2,1)} %get-tuple-element.11) | data formatting | bytes 262144
  130.8 1.5 %copy.18 = bf16[2,16,1024]{2,1,0:T(8,128)(2,1)} copy(bf16[2,16,1024]{2,1,0:T(8,128)(2,1)} %get-tuple-element.12) | data formatting | bytes 131072
  132.2 1.9 %copy.19 = bf16[4,8,2,16,256]{4,3,2,1,0:T(8,128)(2,1)} copy(bf16[4,8,2,16,256]{4,3,2,1,0:T(8,128)(2,1)} %get-tuple-element.13) | data formatting | bytes 1048576
  134.1 1.5 %copy.20 = bf16[2,64,256]{2,1,0:T(8,128)(2,1)} copy(bf16[2,64,256]{2,1,0:T(8,128)(2,1)} %get-tuple-element.14) | data formatting | bytes 131072

commit v2 on v1

--- a/solution.py
+++ b/solution.py
@@ -18,6 +18,7 @@
 HALF = 4
 SHARDS = 16
 COPIES = 96
+SHIFTS = 6
 
 
 def dot(left, right, left_dim, right_dim):
@@ -40,8 +41,8 @@
     out_hbm, in_grad_hbm, expand_grad_hbm, section_grad_hbm, contract_grad_hbm,
     tok, cot, expand_w, section_w, contract_w, chosen, paired, grads, act, hidden, total, gelu_grad,
     u_out, u_in, part_s, part_c, part_e, r1_s, r1_c, r1_e, r2_s, r2_c, r2_e, r3_s, r3_c, r3_e,
-    fin_s, fin_c, fin_e, far_s, far_c, far_e, out_v, in_grad_v,
-    send_sem, recv_sem, local_sem,
+    fin_s, fin_c, fin_e, far_s, far_c, far_e, out_v, in_grad_v, out_back, in_grad_back,
+    send_sem, recv_sem, local_sem, shift_send, shift_recv, shift_local,
 ):
     dp, mp = lax.axis_index("dp"), lax.axis_index("mp")
     core = mp % 2
@@ -57,6 +58,13 @@
     across = [
         (dp, mp + 2**k - 2 * 2**k * ((mp // 2**k) % 2)) for k in range(SECTIONS)
     ]
+    z_low = (mp // 2) % 2
+    before, after = (zh + 3) % 4, (zh + 1) % 4
+    to_before, to_after = (before * 4 + y, mp), (after * 4 + y, mp)
+    other_way = (
+        (before + z_low * (after - before)) * 4 + y,
+        mp + 2 - 4 * z_low,
+    )
     half = (y + y // 2) % 2 * (1 - core) + y // 2 * core
     mine, theirs = half * HALF, (1 - half) * HALF
 
@@ -93,17 +101,63 @@
         sends.append(copy)
         return copy
 
-    tok_in = [load(tokens_hbm.at[:, pl.ds(j * BLK, BLK)], tok.at[j, pl.ds(0, ROWS)]) for j in range(2)]
+    class Shift:
+        def __init__(self, at, src, dst, device):
+            self.near = pltpu.make_async_copy(src, dst, shift_local.at[at])
+            self.far = pltpu.make_async_remote_copy(
+                src_ref=src,
+                dst_ref=dst,
+                send_sem=shift_send.at[at],
+                recv_sem=shift_recv.at[at],
+                device_id=device,
+                device_id_type=MESH,
+            )
+
+            @pl.when(z_low == 0)
+            def _():
+                self.near.start()
+
+            @pl.when(z_low == 1)
+            def _():
+                self.far.start()
+
+        def wait(self):
+            @pl.when(z_low == 0)
+            def _():
+                self.near.wait()
+
+            @pl.when(z_low == 1)
+            def _():
+                self.far.wait_recv()
+
+        def sent(self):
+            @pl.when(z_low == 1)
+            def _():
+                self.far.wait_send()
+
+    tok_in = [load(tokens_hbm.at[pl.ds(0, PIECE), pl.ds(j * BLK, BLK)], tok.at[j, pl.ds(0, PIECE)]) for j in range(2)]
     expand_in = load(expand_hbm, expand_w)
     section_in = [load(section_hbm.at[0], section_w.at[0])]
-    cot_in = [load(cot_hbm.at[:, pl.ds(j * BLK, BLK)], cot.at[j, pl.ds(0, ROWS)]) for j in range(2)]
+    cot_in = [load(cot_hbm.at[pl.ds(0, PIECE), pl.ds(j * BLK, BLK)], cot.at[j, pl.ds(0, PIECE)]) for j in range(2)]
     contract_in = load(contract_hbm, contract_w)
     section_in += [load(section_hbm.at[k], section_w.at[k]) for k in range(1, SECTIONS)]
 
     barrier = pltpu.get_barrier_semaphore()
-    peers = [*across, to_ya, to_yb, to_za, to_zb]
+    peers = [*across, other_way, to_ya, to_yb, to_za, to_zb]
     for device in peers:
         pl.semaphore_signal(barrier, inc=1, device_id=device, device_id_type=MESH)
+
+    pl.semaphore_wait(barrier, len(peers))
+    shifts = [
+        Shift(
+            2 * at + j,
+            src.at[pl.ds(PIECE, PIECE), pl.ds(j * BLK, BLK)],
+            dst.at[j, pl.ds(PIECE, PIECE)],
+            to_before,
+        )
+        for at, (src, dst) in enumerate(((tokens_hbm, tok), (cot_hbm, cot)))
+        for j in range(2)
+    ]
 
     inverse = []
     for k in range(SECTIONS):
@@ -130,9 +184,14 @@
         for m in range(HIDDEN):
             chosen[k, m, rows(piece)] = hidden[pattern[k, m], rows(piece)]
 
+    def partner(k, piece):
+        return other_way if k == 1 and piece == 1 else across[k]
+
     def exchange(k, piece):
         return send(
-            chosen.at[k, :, rows(piece)], paired.at[k, :, rows(piece)], across[k]
+            chosen.at[k, :, rows(piece)],
+            paired.at[k, :, rows(piece)],
+            partner(k, piece),
         )
 
     def own_part(k, piece):
@@ -170,9 +229,14 @@
 
         return use
 
-    def share(ref):
+    def share(ref, first=0, count=ROWS):
         part = ref.at[pl.ds(theirs, HALF)]
-        return send(part.at[:, pl.ds(0, ROWS)], part.at[:, pl.ds(ROWS, ROWS)], to_ya)
+        return send(
+            part.at[:, pl.ds(first, count)], part.at[:, pl.ds(ROWS + first, count)], to_ya
+        )
+
+    def share_piece(name, ref, piece):
+        shared.setdefault(name, []).append(share(ref, piece * PIECE, PIECE))
 
     def share_feature(ref):
         part = ref.at[1 - half]
@@ -185,7 +249,7 @@
             ).astype(BF16)
 
         each(HIDDEN, 4, far)
-        copy = send(u_out.at[k, :, rows(piece)], u_in.at[k, :, rows(piece)], across[k])
+        copy = send(u_out.at[k, :, rows(piece)], u_in.at[k, :, rows(piece)], partner(k, piece))
 
         def near(b):
             total[b, rows(piece)] = dot(
@@ -282,10 +346,11 @@
         copy.wait()
     expand_in.wait()
     for piece in pieces:
+        if piece == 1:
+            for shift in shifts[:2]:
+                shift.wait()
         expand(piece)
         choose(0, piece)
-        if piece == 0:
-            pl.semaphore_wait(barrier, len(peers))
         coming[piece] = exchange(0, piece)
         if piece == 0:
             section_in[0].wait()
@@ -303,7 +368,7 @@
         shared["pair", k] = share(paired.at[k])
         shared["own", k + 1] = share(chosen.at[k + 1])
         if k == 0:
-            for copy in cot_in:
+            for copy in [*cot_in, *shifts[2:]]:
                 copy.wait()
             contract_in.wait()
             shared["cot"] = share_feature(cot)
@@ -319,11 +384,11 @@
 
     for piece in pieces:
         coming[piece].wait_recv()
+        share_piece(("pair", SECTIONS - 1), paired.at[SECTIONS - 1], piece)
         pair_part(SECTIONS - 1, piece, to_gelu(piece))
         coming[piece] = back(SECTIONS - 1, piece)
-    shared["grad", SECTIONS] = share(grads.at[SECTIONS])
-    shared["act"] = share(act)
-    shared["pair", SECTIONS - 1] = share(paired.at[SECTIONS - 1])
+        share_piece("act", act, piece)
+        share_piece(("grad", SECTIONS), grads.at[SECTIONS], piece)
 
     def outputs(j):
         sums = sum(
@@ -333,24 +398,35 @@
         out_v[j] = sums.astype(BF16)
 
     each(2, 1, outputs)
-    for j in range(2):
-        load(out_v.at[j], out_hbm.at[:, pl.ds(j * BLK, BLK)])
+
+    def hand_back(at, ref, back_ref, result):
+        for j in range(2):
+            load(ref.at[j, rows(0)], result.at[rows(0), pl.ds(j * BLK, BLK)])
+        return Shift(at, ref.at[:, rows(1)], back_ref, to_after)
+
+    def take_back(shift, back_ref, result):
+        shift.wait()
+        for j in range(2):
+            load(back_ref.at[j], result.at[rows(1), pl.ds(j * BLK, BLK)])
+
+    shifts.append(hand_back(4, out_v, out_back, out_hbm))
 
     def await_shared(*names):
         for name in names:
-            shared[name].wait_recv()
+            copies = shared[name]
+            for copy in copies if isinstance(copies, list) else [copies]:
+                copy.wait_recv()
 
     def section_first(k):
         await_shared(("grad", k + 1), ("own", k), ("pair", k))
         section_terms(k)
 
-    def stage(k):
-        for piece in pieces:
-            coming[piece].wait_recv()
-            gather_back(k, piece)
-            if k:
-                coming[piece] = back(k - 1, piece)
-        shared["grad", k] = share(grads.at[k])
+    def step(k, piece):
+        coming[piece].wait_recv()
+        gather_back(k, piece)
+        if k:
+            coming[piece] = back(k - 1, piece)
+        share_piece(("grad", k), grads.at[k], piece)
 
     def own_grad(k):
         return section_grad_hbm.at[k, pl.ds(mine, HALF)]
@@ -358,54 +434,67 @@
     def far_grad(k):
         return section_grad_hbm.at[k, pl.ds(theirs, HALF)]
 
-    stage(3)
+    step(3, 0)
     await_shared("act", "cot")
     contract_terms()
     section_first(3)
-    stage(2)
+    step(3, 1)
     reduce_c.second()
+    step(2, 0)
     section_first(2)
+    step(2, 1)
     reduce_s[3].second()
-    stage(1)
-    stage(0)
     reduce_c.third()
+    step(1, 0)
+    section_first(1)
+    step(1, 1)
+    step(0, 0)
+    step(0, 1)
+    reduce_s[2].second()
     reduce_s[3].third()
-    section_first(1)
-    reduce_s[2].second()
+    reduce_c.fourth(contract_grad_hbm.at[half])
     section_first(0)
-    await_shared("tok")
-    await_shared(("grad", 0))
+    reduce_s[1].second()
+    await_shared("tok", ("grad", 0))
     expand_terms()
+    reduce_s[2].third()
+    reduce_s[3].fourth(own_grad(3))
+    reduce_s[0].second()
+    reduce_e.second()
+    take_back(shifts[4], out_back, out_hbm)
     for j in range(2):
         sums = sum(
             dot(grads[0, j * 4 + i, pl.ds(0, ROWS)], expand_w[j, :, i * BLK : (i + 1) * BLK], 1, 1)
             for i in range(4)
         )
         in_grad_v[j] = sums.astype(BF16)
-        load(in_grad_v.at[j], in_grad_hbm.at[:, pl.ds(j * BLK, BLK)])
-    reduce_s[2].third()
-    reduce_c.fourth(contract_grad_hbm.at[half])
-    reduce_s[3].fourth(own_grad(3))
-    reduce_s[1].second()
-    reduce_s[0].second()
-    reduce_e.second()
+    shifts.append(hand_back(5, in_grad_v, in_grad_back, in_grad_hbm))
+    reduce_s[1].third()
+    reduce_c.fifth(contract_grad_hbm.at[1 - half])
     reduce_s[2].fourth(own_grad(2))
-    reduce_s[1].third()
     reduce_s[0].third()
     reduce_e.third()
-    reduce_c.fifth(contract_grad_hbm.at[1 - half])
+    reduce_s[1].fourth(own_grad(1))
     reduce_s[3].fifth(far_grad(3))
-    reduce_s[1].fourth(own_grad(1))
+    take_back(shifts[5], in_grad_back, in_grad_hbm)
     reduce_s[0].fourth(own_grad(0))
+    reduce_s[2].fifth(far_grad(2))
     reduce_e.fourth(expand_grad_hbm.at[half])
-    reduce_s[2].fifth(far_grad(2))
     reduce_s[1].fifth(far_grad(1))
     reduce_s[0].fifth(far_grad(0))
     reduce_e.fifth(expand_grad_hbm.at[1 - half])
+    for shift in shifts:
+        shift.sent()
     for copy in sends:
         copy.wait_send()
     for copy in loads[len(tok_in) + len(cot_in) + 2 + SECTIONS :]:
         copy.wait()
+
+
+def hand_over(*refs):
+    count = len(refs) // 2
+    for at in range(count):
+        refs[count + at][...] = refs[at][...]
 
 
 def body(tokens, expand_weight, section_weight, contract_weight, pattern, cotangent):
@@ -436,20 +525,25 @@
         lead = (count,) if count > 1 else ()
         scratch += [vmem(SECTIONS, *lead, *sec), vmem(*lead, *con), vmem(*lead, *exp)]
     scratch += [vmem(2, ROWS, BLK), vmem(2, ROWS, BLK)]
+    scratch += [vmem(2, PIECE, BLK), vmem(2, PIECE, BLK)]
     scratch += [
         pltpu.SemaphoreType.DMA((COPIES,)),
         pltpu.SemaphoreType.DMA((COPIES,)),
         pltpu.SemaphoreType.DMA((COPIES,)),
+        pltpu.SemaphoreType.DMA((SHIFTS,)),
+        pltpu.SemaphoreType.DMA((SHIFTS,)),
+        pltpu.SemaphoreType.DMA((SHIFTS,)),
     ]
-    return pl.pallas_call(
+    shapes = (
+        jax.ShapeDtypeStruct((ROWS, 2 * BLK), BF16),
+        jax.ShapeDtypeStruct((ROWS, 2 * BLK), BF16),
+        jax.ShapeDtypeStruct((2, 16, 4 * BLK), BF16),
+        jax.ShapeDtypeStruct((SECTIONS, HIDDEN, 2, 16, BLK), BF16),
+        jax.ShapeDtypeStruct((2, 64, BLK), BF16),
+    )
+    results = pl.pallas_call(
         lambda *refs: kernel(scale, *refs),
-        out_shape=(
-            jax.ShapeDtypeStruct((ROWS, 2 * BLK), BF16),
-            jax.ShapeDtypeStruct((ROWS, 2 * BLK), BF16),
-            jax.ShapeDtypeStruct((2, 16, 4 * BLK), BF16),
-            jax.ShapeDtypeStruct((SECTIONS, HIDDEN, 2, 16, BLK), BF16),
-            jax.ShapeDtypeStruct((2, 64, BLK), BF16),
-        ),
+        out_shape=shapes,
         in_specs=[pl.BlockSpec(memory_space=pltpu.SMEM)] + [hbm] * 5,
         out_specs=(hbm,) * 5,
         scratch_shapes=scratch,
@@ -458,6 +552,14 @@
         ),
         name="butterfly",
     )(pattern, tokens, expand_weight, section_weight, contract_weight, cotangent)
+    whole = pl.BlockSpec(memory_space=pltpu.VMEM)
+    return pl.pallas_call(
+        hand_over,
+        out_shape=shapes,
+        in_specs=[whole] * 5,
+        out_specs=(whole,) * 5,
+        name="hand_over",
+    )(*results)
 
 
 def solution(mesh):

time: 136 us -> 128 us (0.941)
  local copies, waits for them, and re-layouts: 7.95 us -> 0 us
    unnamed x5 -> x0, local copies, waits for them, and re-layouts: 7.95 us -> none
    pallas_call x1 -> x2, Pallas kernels: 127 us -> 126 us  [the longest x1 124 us: body(): pl.pallas_call(lambda *refs: kernel(scale, *refs), out_shape=shapes, in_s...]
where the time goes in v2:
time: 128 us; the launch traced here: 127 us
  Pallas kernels  126 us (98%)
    pallas_call x1, Pallas kernels, body(): pl.pallas_call(lambda *refs: kernel(scale, *refs), out_shape=shapes, in_s...  124 us

profile of v2, /device:TPU:1, one launch (start us, length us, event | category | flops | bytes accessed | tf_op | source)
XLA Modules:
  0.0 127.1 jit_solution(5338564474151321431)
XLA Ops:
  0.6 124.4 %butterfly.1 = (bf16[128,512]{1,0:T(8,128)(2,1)}, bf16[128,512]{1,0:T(8,128)(2,1)}, bf16[2,16,1024]{2,1,0:T(8,128)(2,1)}, bf16[4,8,2,16,256]{4,3,2,1,0:T(8,128)(2,1)}, bf16[2,64,256]{2,1,0:T(8,128)(2,1)}) custom-call(s32[4,8]{1,0:T(4,128)} %refs_0_.1, bf16[128,512]{1,0:T(8,128)(2,1)} %refs_1_.1, bf16[2,256,1024]{2,1,0:T(8,128)(2,1)} %refs_2_.1, ...), custom_call_target="tpu_custom_call" | custom-call | tf_op jit(solution)/shard_map/butterfly/pallas_call | solution.py:544
  125.1 2.1 %hand_over.1 = (bf16[128,512]{1,0:T(8,128)(2,1)}, bf16[128,512]{1,0:T(8,128)(2,1)}, bf16[2,16,1024]{2,1,0:T(8,128)(2,1)}, bf16[4,8,2,16,256]{4,3,2,1,0:T(8,128)(2,1)}, bf16[2,64,256]{2,1,0:T(8,128)(2,1)}) custom-call(bf16[128,512]{1,0:T(8,128)(2,1)} %get-tuple-element.10.refs_0_, bf16[128,512]{1,0:T(8,128)(2,1)} %get-tuple-element.11.refs_1_, ...), custom_call_target="tpu_custom_call" | custom-call | tf_op jit(solution)/shard_map/hand_over/pallas_call | solution.py:556

commit v3 on v2

--- a/solution.py
+++ b/solution.py
@@ -308,10 +308,36 @@
             self.copy.wait_recv()
             load(self.far, other)
 
-    reduce_s = [
-        Reduction(part_s.at[k], r1_s.at[k], r2_s.at[k], r3_s.at[k], fin_s.at[k], far_s.at[k], 1)
-        for k in range(SECTIONS)
-    ]
+    class Sections:
+        def __init__(self, k):
+            self.k, self.halves = k, []
+            for h in range(2):
+                part = pl.ds(2 * h, 2)
+                self.halves.append(
+                    Reduction(
+                        *(ref.at[k, :, part] for ref in (part_s, r1_s, r2_s, r3_s, fin_s)),
+                        far_s.at[k, part],
+                        2,
+                    )
+                )
+
+        def second(self):
+            for one in self.halves:
+                one.second()
+
+        def third(self):
+            for one in self.halves:
+                one.third()
+
+        def fourth(self):
+            for h, one in enumerate(self.halves):
+                one.fourth(section_grad_hbm.at[self.k, pl.ds(mine + 2 * h, 2)])
+
+        def fifth(self):
+            for h, one in enumerate(self.halves):
+                one.fifth(section_grad_hbm.at[self.k, pl.ds(theirs + 2 * h, 2)])
+
+    reduce_s = [Sections(k) for k in range(SECTIONS)]
     reduce_c = Reduction(part_c, r1_c, r2_c, r3_c, fin_c, far_c, 2)
     reduce_e = Reduction(part_e, r1_e, r2_e, r3_e, fin_e, far_e, 2)
 
@@ -322,7 +348,8 @@
                 term = dot(ref[k, mine + i], upstream, 0, 0).astype(BF16)
                 for shard in range(SHARDS):
                     part_s[k, slot[shard], i, s] = term[shard * 16 : (shard + 1) * 16]
-        reduce_s[k].first()
+            if i % 2:
+                reduce_s[k].halves[i // 2].first()
 
     def contract_terms():
         for i in range(HALF):
@@ -428,12 +455,6 @@
             coming[piece] = back(k - 1, piece)
         share_piece(("grad", k), grads.at[k], piece)
 
-    def own_grad(k):
-        return section_grad_hbm.at[k, pl.ds(mine, HALF)]
-
-    def far_grad(k):
-        return section_grad_hbm.at[k, pl.ds(theirs, HALF)]
-
     step(3, 0)
     await_shared("act", "cot")
     contract_terms()
@@ -458,7 +479,7 @@
     await_shared("tok", ("grad", 0))
     expand_terms()
     reduce_s[2].third()
-    reduce_s[3].fourth(own_grad(3))
+    reduce_s[3].fourth()
     reduce_s[0].second()
     reduce_e.second()
     take_back(shifts[4], out_back, out_hbm)
@@ -471,17 +492,17 @@
     shifts.append(hand_back(5, in_grad_v, in_grad_back, in_grad_hbm))
     reduce_s[1].third()
     reduce_c.fifth(contract_grad_hbm.at[1 - half])
-    reduce_s[2].fourth(own_grad(2))
+    reduce_s[2].fourth()
     reduce_s[0].third()
     reduce_e.third()
-    reduce_s[1].fourth(own_grad(1))
-    reduce_s[3].fifth(far_grad(3))
+    reduce_s[1].fourth()
+    reduce_s[3].fifth()
     take_back(shifts[5], in_grad_back, in_grad_hbm)
-    reduce_s[0].fourth(own_grad(0))
-    reduce_s[2].fifth(far_grad(2))
+    reduce_s[0].fourth()
+    reduce_s[2].fifth()
     reduce_e.fourth(expand_grad_hbm.at[half])
-    reduce_s[1].fifth(far_grad(1))
-    reduce_s[0].fifth(far_grad(0))
+    reduce_s[1].fifth()
+    reduce_s[0].fifth()
     reduce_e.fifth(expand_grad_hbm.at[1 - half])
     for shift in shifts:
         shift.sent()

time: 128 us -> 127 us (level)
  no operation moved by 1% of the time
where the time goes in v3:
time: 127 us; the launch traced here: 126 us
  Pallas kernels  126 us (99%)
    pallas_call x1, Pallas kernels, body(): pl.pallas_call(lambda *refs: kernel(scale, *refs), out_shape=shapes, in_s...  124 us

profile of v3, /device:TPU:1, one launch (start us, length us, event | category | flops | bytes accessed | tf_op | source)
XLA Modules:
  0.0 126.5 jit_solution(12809768238502001066)
XLA Ops:
  0.6 123.8 %butterfly.1 = (bf16[128,512]{1,0:T(8,128)(2,1)}, bf16[128,512]{1,0:T(8,128)(2,1)}, bf16[2,16,1024]{2,1,0:T(8,128)(2,1)}, bf16[4,8,2,16,256]{4,3,2,1,0:T(8,128)(2,1)}, bf16[2,64,256]{2,1,0:T(8,128)(2,1)}) custom-call(s32[4,8]{1,0:T(4,128)} %refs_0_.1, bf16[128,512]{1,0:T(8,128)(2,1)} %refs_1_.1, bf16[2,256,1024]{2,1,0:T(8,128)(2,1)} %refs_2_.1, ...), custom_call_target="tpu_custom_call" | custom-call | tf_op jit(solution)/shard_map/butterfly/pallas_call | solution.py:565
  124.4 2.1 %hand_over.1 = (bf16[128,512]{1,0:T(8,128)(2,1)}, bf16[128,512]{1,0:T(8,128)(2,1)}, bf16[2,16,1024]{2,1,0:T(8,128)(2,1)}, bf16[4,8,2,16,256]{4,3,2,1,0:T(8,128)(2,1)}, bf16[2,64,256]{2,1,0:T(8,128)(2,1)}) custom-call(bf16[128,512]{1,0:T(8,128)(2,1)} %get-tuple-element.10.refs_0_, bf16[128,512]{1,0:T(8,128)(2,1)} %get-tuple-element.11.refs_1_, ...), custom_call_target="tpu_custom_call" | custom-call | tf_op jit(solution)/shard_map/hand_over/pallas_call | solution.py:577
